TPU v7x, 32 devices: a whole 2x2x4 slice. The times are simulated.
32 devices in a mesh: pipe: 8 (over z, y), expert: 4 (over x, core).
Axes of the slice: x: 2, y: 2, z: 4, core: 2. Of those that a mesh axis runs over, the one named last changes fastest.
Arguments:
- up_in: bfloat16 [8, 256, 2560], P('pipe', 'expert'), may hold values from -6 to 6
- down_in: bfloat16 [8, 256, 2560], P('pipe', 'expert'), may hold values from -6 to 6
- up_ids: int32 [8, 256, 6], P('pipe', 'expert'), may hold values from 0 to 15, all different within a row; in each aligned block of 64 rows (0 to 63, 64 to 127, ..., all dimensions but the last counted through in order) at most 32 rows name the same one
- down_ids: int32 [8, 256, 6], P('pipe', 'expert'), may hold values from 0 to 15, all different within a row; in each aligned block of 64 rows (0 to 63, 64 to 127, ..., all dimensions but the last counted through in order) at most 32 rows name the same one
- norm_gain: float32 [8, 2560], P('pipe'), may hold values from 0.1 to 1.9
- router: bfloat16 [8, 2560, 16], P('pipe'), may hold values from -0.25 to 0.25
- w_up: bfloat16 [8, 16, 2560, 1152], P('pipe', 'expert'), may hold values from -0.125 to 0.125
- w_down: bfloat16 [8, 16, 1152, 2560], P('pipe', 'expert'), may hold values from -0.375 to 0.375
Outputs:
- up_out: bfloat16 [8, 256, 2560], P('pipe', 'expert')
- down_out: bfloat16 [8, 256, 2560], P('pipe', 'expert')
Inputs may be any that keep to these rules, and one draw needn't show every extreme that they name: `up_ids`: each token names 6 different experts. Within the tokens of one device (aligned blocks of 64 tokens of one section) no expert is named more than 32 times, and in every draw some expert is named exactly 32 times in some block. `down_ids`: as for up_ids.
All inputs are finite; a program needn't handle non-finite values.
Results may differ from a plain program's by a relative error of at most 0.0061.
Values may be sent and summed in bfloat16 or wider, within the bound.
A program may use at most 128 MiB of HBM per device.

v0:
```python
import jax
import jax.numpy as jnp
from jax import lax
from jax.sharding import PartitionSpec as P

CAP = 32


def shifted(block, axis, distance):
    devices = range(lax.axis_size(axis))
    route = [((i - distance) % len(devices), i) for i in devices]
    return lax.ppermute(block, axis, route)


def layer_route(x, ids, gain, table, owners_count):
    tokens_here = x.shape[0]
    experts = table.shape[1]
    width = x.shape[1]
    choose = ids.shape[1]
    xf = x.astype(jnp.float32)
    normed = (xf * lax.rsqrt(jnp.mean(xf * xf, axis=-1, keepdims=True) + 1e-06) * gain).astype(
        jnp.bfloat16
    )
    logits = jnp.dot(normed, table, preferred_element_type=jnp.float32)
    onehot = (ids[:, :, None] == jnp.arange(experts, dtype=jnp.int32)[None, None, :]).astype(
        jnp.int32
    )
    chosen = jnp.take_along_axis(logits, ids, axis=1)
    score = jax.nn.sigmoid(chosen)
    gates = score / jnp.sum(score, axis=-1, keepdims=True)
    flat = onehot.reshape(tokens_here * choose, experts)
    before = jnp.cumsum(flat, axis=0) - flat
    slot = jnp.sum(before * flat, axis=-1)
    target = ids.reshape(-1) * CAP + slot
    token_of = jnp.arange(tokens_here * choose, dtype=jnp.int32) // choose + 1
    source_row = jnp.zeros((experts * CAP,), jnp.int32).at[target].set(token_of)
    padded = jnp.concatenate([jnp.zeros((1, width), jnp.bfloat16), normed], axis=0)
    send = jnp.take(padded, source_row, axis=0)
    send = send.reshape(owners_count, experts // owners_count, CAP, width)
    return (send, target, gates)


def apply_experts(rows, up_w, down_w):
    up_h = jnp.einsum("slcd,ldf->slcf", rows, up_w, preferred_element_type=jnp.float32)
    hidden = jax.nn.silu(up_h).astype(jnp.bfloat16)
    return jnp.einsum("slcf,lfd->slcd", hidden, down_w, preferred_element_type=jnp.float32).astype(
        jnp.bfloat16
    )


def finish(x, gates, returned, target):
    tokens_here, choose = gates.shape
    width = x.shape[1]
    picked = jnp.take(returned.reshape(-1, width), target, axis=0)
    picked = picked.reshape(tokens_here, choose, width).astype(jnp.float32)
    combined = jnp.sum(gates[:, :, None] * picked, axis=1)
    return (x.astype(jnp.float32) + 2.5 * combined).astype(jnp.bfloat16)


def per_device(up_in, down_in, up_ids, down_ids, norm_gain, router, w_up, w_down):
    owners_count = lax.axis_size("expert")
    gain = norm_gain[0]
    table = router[0]
    up_w = w_up[0]
    down_w = w_down[0]
    send_up, target_up, gates_up = layer_route(up_in[0], up_ids[0], gain, table, owners_count)
    send_down, target_down, gates_down = layer_route(
        down_in[0], down_ids[0], gain, table, owners_count
    )

    def run_single(rows):
        return lax.all_to_all(
            apply_experts(rows, up_w, down_w), "expert", split_axis=0, concat_axis=0, tiled=True
        )

    def dispatch_single(send):
        return run_single(lax.all_to_all(send, "expert", split_axis=0, concat_axis=0, tiled=True))

    back_up = dispatch_single(send_up)
    back_down = dispatch_single(send_down)
    layer_up = finish(up_in[0], gates_up, back_up, target_up)
    layer_down = finish(down_in[0], gates_down, back_down, target_down)
    up_out = shifted(layer_up[None], "pipe", 1)
    down_out = shifted(layer_down[None], "pipe", -1)
    return (up_out, down_out)


def solution(mesh):
    placed = (
        P("pipe", "expert", None),
        P("pipe", "expert", None),
        P("pipe", "expert", None),
        P("pipe", "expert", None),
        P("pipe", None),
        P("pipe", None, None),
        P("pipe", "expert", None, None),
        P("pipe", "expert", None, None),
    )
    return jax.shard_map(
        per_device,
        mesh=mesh,
        in_specs=placed,
        out_specs=(P("pipe", "expert", None), P("pipe", "expert", None)),
        check_vma=False,
    )
```

profile of v0, /device:TPU:0, one launch (start us, length us, event | category | flops | bytes accessed | tf_op | source)
XLA Modules:
  0.0 192.2 jit_solution(11101079316984250926)
XLA Ops:
  0.6 0.8 copy.52
  1.7 0.7 broadcast_multiply_fusion
  2.5 0.9 reduce-window.16
  3.3 0.2 slice_reduce_fusion
  3.9 2.9 %scatter_custom_fusion.1 = s32[512]{0:T(512)S(1)} fusion(s32[384]{0:T(512)S(1)} %fusion.81, s32[384]{0:T(512)S(1)} %fusion.76, s32[]{:T(128)} %constant.48.clone.1), kind=kCustom, calls=%fused_computation.123 | custom fusion | bytes 2052 | tf_op jit(solution)/shard_map/scatter | solution.py:36
  6.9 1.1 fusion.40
  8.0 1.1 fusion.43
  9.2 0.7 reduce
  10.0 1.9 %fusion.42 = (bf16[64,2560]{1,0:T(8,128)(2,1)S(1)}, bf16[64,2560]{1,0:T(8,128)(2,1)}) fusion(bf16[1,64,2560]{2,1,0:T(8,128)(2,1)} %param.15, f32[64]{0:T(128)S(1)} %get-tuple-element.11, f32[2560]{0:T(1024)S(1)} %reduce, f32[64]{0:T(128)S(1)} %get-tuple-element.12, bf16[1,64,2560]{2,1,0:T(8,128)(2,1)} %param.14), kind=kLoop, calls=%fused_computation.44 | loop fusion | flops 1310720 | bytes 1321472 | tf_op jit(solution)/shard_map/convert_element_type | solution.py:21
  12.0 2.6 %gather_fusion.4 = bf16[512,2560]{1,0:T(8,128)(2,1)S(1)} fusion(bf16[65,2560]{1,0:T(8,128)(2,1)S(1)} %concatenate.7, s32[1024]{0:T(1024)S(1)} %pad_clamp_fusion.1), kind=kCustom, calls=%fused_computation.4.clone | custom fusion | bytes 5244928 | tf_op jit(solution)/shard_map/jit(_take)/gather | solution.py:38
  14.6 1.8 broadcast_select_fusion
  16.4 4.7 %all-to-all-start.2 = ((bf16[4,4,32,2560]{3,2,1,0:T(8,128)(2,1)}), bf16[4,4,32,2560]{3,2,1,0:T(8,128)(2,1)}, u32[]{:S(2)}, u32[]{:S(2)}) async-start(bf16[4,4,32,2560]{3,2,1,0:T(8,128)(2,1)} %bitcast.20), calls=%async_computation.2 | async-start | bytes 5242880 | tf_op jit(solution)/shard_map/all_to_all | solution.py:77
  21.6 0.3 fusion.53
  21.8 0.3 fusion.56
  22.4 3.0 %gather_fusion.3 = f32[384]{0:T(512)S(1)} fusion(f32[64,16]{0,1:T(8,128)S(1)} %fusion.53, s32[384]{0:T(512)S(1)} %reshape.297), kind=kCustom, calls=%fused_computation.3.clone | custom fusion | bytes 6144 | tf_op jit(solution)/shard_map/jit(take_along_axis)/gather | solution.py:28
  25.6 0.9 reduce-window.14
  27.3 3.0 %gather_fusion = f32[384]{0:T(512)S(1)} fusion(f32[64,16]{0,1:T(8,128)S(1)} %fusion.56, s32[384]{0:T(512)S(1)} %reshape.288), kind=kCustom, calls=%fused_computation.clone | custom fusion | bytes 6144 | tf_op jit(solution)/shard_map/jit(take_along_axis)/gather | solution.py:28
  30.7 2.9 %scatter_custom_fusion = s32[512]{0:T(512)S(1)} fusion(s32[384]{0:T(512)S(1)} %fusion.80, s32[384]{0:T(512)S(1)} %fusion.76, s32[]{:T(128)} %constant.48.clone.1), kind=kCustom, calls=%fused_computation.125 | custom fusion | bytes 2052 | tf_op jit(solution)/shard_map/scatter | solution.py:36
  33.9 2.6 %gather_fusion.1 = bf16[512,2560]{1,0:T(8,128)(2,1)S(1)} fusion(bf16[65,2560]{1,0:T(8,128)(2,1)S(1)} %concatenate.6, s32[1024]{0:T(1024)S(1)} %pad_clamp_fusion.3), kind=kCustom, calls=%fused_computation.1.clone | custom fusion | bytes 5244928 | tf_op jit(solution)/shard_map/jit(_take)/gather | solution.py:38
  36.5 1.8 broadcast_select_fusion.1
  38.4 14.7 %all-to-all-done.2 = bf16[4,4,32,2560]{3,2,1,0:T(8,128)(2,1)} async-done(((bf16[4,4,32,2560]{3,2,1,0:T(8,128)(2,1)}), bf16[4,4,32,2560]{3,2,1,0:T(8,128)(2,1)}, u32[]{:S(2)}, u32[]{:S(2)}) %all-to-all-start.2) | async-done | bytes 2621472 | tf_op jit(solution)/shard_map/all_to_all | solution.py:77
  53.1 3.8 %all-to-all-start = ((bf16[4,4,32,2560]{3,2,1,0:T(8,128)(2,1)}), bf16[4,4,32,2560]{3,2,1,0:T(8,128)(2,1)S(1)}, u32[]{:S(2)}, u32[]{:S(2)}) async-start(bf16[4,4,32,2560]{3,2,1,0:T(8,128)(2,1)} %bitcast.5), calls=%async_computation | async-start | bytes 5242880 | tf_op jit(solution)/shard_map/all_to_all | solution.py:77
  57.0 12.3 %multiply_convert_fusion = bf16[4,4,32,1152]{3,2,0,1:T(8,128)(2,1)S(1)} fusion(bf16[1,4,2560,1152]{3,2,1,0:T(8,128)(2,1)} %param.20, bf16[4,4,32,2560]{3,2,1,0:T(8,128)(2,1)} %all-to-all-done.2), kind=kOutput, calls=%fused_computation.28 | convolution fusion | flops 3022848000 | bytes 27394048 | tf_op jit(solution)/shard_map/slcd,ldf->slcf/dot_general | solution.py:44
  69.3 11.5 %fusion.14 = bf16[4,4,32,2560]{3,2,0,1:T(8,128)(2,1)S(1)} fusion(bf16[4,4,32,1152]{3,2,0,1:T(8,128)(2,1)S(1)} %multiply_convert_fusion, bf16[1,4,1152,2560]{3,2,1,0:T(8,128)(2,1)} %param.21), kind=kOutput, calls=%fused_computation.20 | convolution fusion | flops 3021209600 | bytes 27394048 | tf_op jit(solution)/shard_map/slcf,lfd->slcd/dot_general | solution.py:46
  80.8 1.7 copy.57
  82.5 5.6 %all-to-all-done = bf16[4,4,32,2560]{3,2,1,0:T(8,128)(2,1)S(1)} async-done(((bf16[4,4,32,2560]{3,2,1,0:T(8,128)(2,1)}), bf16[4,4,32,2560]{3,2,1,0:T(8,128)(2,1)S(1)}, u32[]{:S(2)}, u32[]{:S(2)}) %all-to-all-start) | async-done | bytes 2621472 | tf_op jit(solution)/shard_map/all_to_all | solution.py:77
  88.1 1.5 copy-done.6
  89.6 3.9 %all-to-all-start.3 = ((bf16[4,4,32,2560]{3,2,1,0:T(8,128)(2,1)}), bf16[4,4,32,2560]{3,2,1,0:T(8,128)(2,1)S(1)}, u32[]{:S(2)}, u32[]{:S(2)}) async-start(bf16[4,4,32,2560]{3,2,1,0:T(8,128)(2,1)} %copy.57), calls=%async_computation.3 | async-start | bytes 5242880 | tf_op jit(solution)/shard_map/all_to_all | solution.py:72
  93.5 12.3 %multiply_convert_fusion.1 = bf16[4,4,32,1152]{3,2,0,1:T(8,128)(2,1)S(1)} fusion(bf16[1,4,2560,1152]{3,2,1,0:T(8,128)(2,1)} %param.20, bf16[4,4,32,2560]{3,2,1,0:T(8,128)(2,1)} %copy-done.6), kind=kOutput, calls=%fused_computation.29 | convolution fusion | flops 3022848000 | bytes 27394048 | tf_op jit(solution)/shard_map/slcd,ldf->slcf/dot_general | solution.py:44
  105.8 11.5 %fusion.17 = bf16[4,4,32,2560]{3,2,0,1:T(8,128)(2,1)S(1)} fusion(bf16[4,4,32,1152]{3,2,0,1:T(8,128)(2,1)S(1)} %multiply_convert_fusion.1, bf16[1,4,1152,2560]{3,2,1,0:T(8,128)(2,1)} %param.21), kind=kOutput, calls=%fused_computation.21 | convolution fusion | flops 3021209600 | bytes 27394048 | tf_op jit(solution)/shard_map/slcf,lfd->slcd/dot_general | solution.py:46
  117.3 1.7 copy.48
  119.0 5.6 %all-to-all-done.3 = bf16[4,4,32,2560]{3,2,1,0:T(8,128)(2,1)S(1)} async-done(((bf16[4,4,32,2560]{3,2,1,0:T(8,128)(2,1)}), bf16[4,4,32,2560]{3,2,1,0:T(8,128)(2,1)S(1)}, u32[]{:S(2)}, u32[]{:S(2)}) %all-to-all-start.3) | async-done | bytes 2621472 | tf_op jit(solution)/shard_map/all_to_all | solution.py:72
  124.5 1.5 copy-done.2
  126.0 3.9 %all-to-all-start.1 = ((bf16[4,4,32,2560]{3,2,1,0:T(8,128)(2,1)}), bf16[4,4,32,2560]{3,2,1,0:T(8,128)(2,1)S(1)}, u32[]{:S(2)}, u32[]{:S(2)}) async-start(bf16[4,4,32,2560]{3,2,1,0:T(8,128)(2,1)} %copy.48), calls=%async_computation.1 | async-start | bytes 5242880 | tf_op jit(solution)/shard_map/all_to_all | solution.py:72
  130.0 7.9 %gather_fusion.5 = bf16[384,2560]{1,0:T(8,128)(2,1)} fusion(bf16[512,2560]{1,0:T(8,128)(2,1)} %bitcast.158, s32[1024]{0:T(1024)S(1)} %pad_clamp_fusion), kind=kCustom, calls=%fused_computation.5.clone | custom fusion | bytes 3933696 | tf_op jit(solution)/shard_map/jit(_take)/gather | solution.py:54
  137.9 3.8 %select_convert_fusion = f32[384,2560]{1,0:T(8,128)} fusion(bf16[384,2560]{1,0:T(8,128)(2,1)} %gather_fusion.5, pred[384]{0:T(512)(128)(4,1)S(1)} %get-tuple-element.4), kind=kLoop, calls=%fused_computation.30 | loop fusion | flops 1966080 | bytes 5898624 | tf_op jit(solution)/shard_map/convert_element_type | solution.py:55
  141.7 5.1 %reshape.212 = f32[64,6,2560]{2,1,0:T(8,128)} reshape(f32[384,2560]{1,0:T(8,128)} %select_convert_fusion) | data formatting | bytes 7864320 | tf_op jit(solution)/shard_map/convert_element_type | solution.py:55
  146.8 4.4 %multiply_reduce_fusion = f32[64,2560]{1,0:T(8,128)S(1)} fusion(f32[64,6,2560]{2,1,0:T(8,128)} %reshape.212, f32[64,6]{1,0:T(8,128)S(1)} %copy.51), kind=kLoop, calls=%fused_computation.16 | loop fusion | flops 1802240 | bytes 4589056 | tf_op jit(solution)/shard_map/reduce_sum | solution.py:56
  151.4 5.4 %collective-permute-start.1 = (bf16[1,64,2560]{2,1,0:T(8,128)(2,1)S(1)}, bf16[1,64,2560]{2,1,0:T(8,128)(2,1)S(1)}, u32[]{:S(2)}, u32[]{:S(2)}) collective-permute-start(bf16[1,64,2560]{2,1,0:T(8,128)(2,1)S(1)} %fusion.51), channel_id=1, source_target_pairs={{4,0},{8,4},{12,8},{16,12},{20,16},{24,20},{28,24},{0,28},{5,1},{9... | collective-permute-start | bytes 983048 | tf_op jit(solution)/shard_map/ppermute | solution.py:12
  156.8 4.2 %all-to-all-done.1 = bf16[4,4,32,2560]{3,2,1,0:T(8,128)(2,1)S(1)} async-done(((bf16[4,4,32,2560]{3,2,1,0:T(8,128)(2,1)}), bf16[4,4,32,2560]{3,2,1,0:T(8,128)(2,1)S(1)}, u32[]{:S(2)}, u32[]{:S(2)}) %all-to-all-start.1) | async-done | bytes 2621472 | tf_op jit(solution)/shard_map/all_to_all | solution.py:72
  161.0 3.3 %gather_fusion.2 = bf16[384,2560]{1,0:T(8,128)(2,1)} fusion(bf16[512,2560]{1,0:T(8,128)(2,1)S(1)} %bitcast.157, s32[1024]{0:T(1024)S(1)} %pad_clamp_fusion.2), kind=kCustom, calls=%fused_computation.2.clone | custom fusion | bytes 3933696 | tf_op jit(solution)/shard_map/jit(_take)/gather | solution.py:54
  164.3 3.8 %select_convert_fusion.1 = f32[384,2560]{1,0:T(8,128)} fusion(bf16[384,2560]{1,0:T(8,128)(2,1)} %gather_fusion.2, pred[384]{0:T(512)(128)(4,1)S(1)} %get-tuple-element.7), kind=kLoop, calls=%fused_computation.31 | loop fusion | flops 1966080 | bytes 5898624 | tf_op jit(solution)/shard_map/convert_element_type | solution.py:55
  168.1 5.1 %reshape.210 = f32[64,6,2560]{2,1,0:T(8,128)} reshape(f32[384,2560]{1,0:T(8,128)} %select_convert_fusion.1) | data formatting | bytes 7864320 | tf_op jit(solution)/shard_map/convert_element_type | solution.py:55
  173.2 4.5 %multiply_reduce_fusion.1 = f32[64,2560]{1,0:T(8,128)S(1)} fusion(f32[64,6,2560]{2,1,0:T(8,128)} %reshape.210, f32[64,6]{1,0:T(8,128)S(1)} %copy.42), kind=kLoop, calls=%fused_computation.17 | loop fusion | flops 1802240 | bytes 4589056 | tf_op jit(solution)/shard_map/reduce_sum | solution.py:56
  177.8 2.4 %collective-permute-start = (bf16[1,64,2560]{2,1,0:T(8,128)(2,1)S(1)}, bf16[1,64,2560]{2,1,0:T(8,128)(2,1)S(1)}, u32[]{:S(2)}, u32[]{:S(2)}) collective-permute-start(bf16[1,64,2560]{2,1,0:T(8,128)(2,1)S(1)} %fusion.48), channel_id=1, source_target_pairs={{28,0},{0,4},{4,8},{8,12},{12,16},{16,20},{20,24},{24,28},{29,1},{... | collective-permute-start | bytes 983048 | tf_op jit(solution)/shard_map/ppermute | solution.py:12
  180.2 10.5 %collective-permute-done = bf16[1,64,2560]{2,1,0:T(8,128)(2,1)S(1)} collective-permute-done((bf16[1,64,2560]{2,1,0:T(8,128)(2,1)S(1)}, bf16[1,64,2560]{2,1,0:T(8,128)(2,1)S(1)}, u32[]{:S(2)}, u32[]{:S(2)}) %collective-permute-start) | collective-permute-done | bytes 327712 | tf_op jit(solution)/shard_map/ppermute | solution.py:12
  190.7 0.7 copy.94
  191.4 0.7 copy.95
  (70 shorter events, 3.3 us)
Async XLA Ops:
  0.6 20.9 %copy-start = (bf16[1,2560,16]{1,2,0:T(8,128)(2,1)S(1)}, bf16[1,2560,16]{1,2,0:T(8,128)(2,1)}, u32[]{:S(2)}) copy-start(bf16[1,2560,16]{1,2,0:T(8,128)(2,1)} %param.19) | copy-start | bytes 245764
  16.4 4.7 %copy-start.8 = (s32[1,64,6]{1,0,2:T(1,128)S(1)}, s32[1,64,6]{1,0,2:T(1,128)}, u32[]{:S(2)}) copy-start(s32[1,64,6]{1,0,2:T(1,128)} %param.17) | copy-start | bytes 4612
  16.4 4.7 %copy-start.9 = (s32[1,64,6]{1,0,2:T(1,128)S(1)}, s32[1,64,6]{1,0,2:T(1,128)}, u32[]{:S(2)}) copy-start(s32[1,64,6]{1,0,2:T(1,128)} %param.16) | copy-start | bytes 4612
  16.4 5.1 %copy-start.3 = (bf16[1,64,2560]{2,1,0:T(8,128)(2,1)S(1)}, bf16[1,64,2560]{2,1,0:T(8,128)(2,1)}, u32[]{:S(2)}) copy-start(bf16[1,64,2560]{2,1,0:T(8,128)(2,1)} %param.15) | copy-start | bytes 983044
  16.4 5.4 %copy-start.4 = (bf16[1,64,2560]{2,1,0:T(8,128)(2,1)S(1)}, bf16[1,64,2560]{2,1,0:T(8,128)(2,1)}, u32[]{:S(2)}) copy-start(bf16[1,64,2560]{2,1,0:T(8,128)(2,1)} %param.14) | copy-start | bytes 983044
  16.4 36.7 %all-to-all-start.2 = ((bf16[4,4,32,2560]{3,2,1,0:T(8,128)(2,1)}), bf16[4,4,32,2560]{3,2,1,0:T(8,128)(2,1)}, u32[]{:S(2)}, u32[]{:S(2)}) async-start(bf16[4,4,32,2560]{3,2,1,0:T(8,128)(2,1)} %bitcast.20), calls=%async_computation.2 | async-start | bytes 5242880 | tf_op jit(solution)/shard_map/all_to_all | solution.py:77
  27.2 6.4 %copy-start.7 = (bf16[64,2560]{1,0:T(8,128)(2,1)S(1)}, bf16[64,2560]{1,0:T(8,128)(2,1)}, u32[]{:S(2)}) copy-start(bf16[64,2560]{1,0:T(8,128)(2,1)} %get-tuple-element.10) | copy-start | bytes 983044
  53.1 34.9 %all-to-all-start = ((bf16[4,4,32,2560]{3,2,1,0:T(8,128)(2,1)}), bf16[4,4,32,2560]{3,2,1,0:T(8,128)(2,1)S(1)}, u32[]{:S(2)}, u32[]{:S(2)}) async-start(bf16[4,4,32,2560]{3,2,1,0:T(8,128)(2,1)} %bitcast.5), calls=%async_computation | async-start | bytes 5242880 | tf_op jit(solution)/shard_map/all_to_all | solution.py:77
  88.1 1.5 copy-start.6
  89.6 34.9 %all-to-all-start.3 = ((bf16[4,4,32,2560]{3,2,1,0:T(8,128)(2,1)}), bf16[4,4,32,2560]{3,2,1,0:T(8,128)(2,1)S(1)}, u32[]{:S(2)}, u32[]{:S(2)}) async-start(bf16[4,4,32,2560]{3,2,1,0:T(8,128)(2,1)} %copy.57), calls=%async_computation.3 | async-start | bytes 5242880 | tf_op jit(solution)/shard_map/all_to_all | solution.py:72
  124.5 1.5 copy-start.2
  126.0 34.9 %all-to-all-start.1 = ((bf16[4,4,32,2560]{3,2,1,0:T(8,128)(2,1)}), bf16[4,4,32,2560]{3,2,1,0:T(8,128)(2,1)S(1)}, u32[]{:S(2)}, u32[]{:S(2)}) async-start(bf16[4,4,32,2560]{3,2,1,0:T(8,128)(2,1)} %copy.48), calls=%async_computation.1 | async-start | bytes 5242880 | tf_op jit(solution)/shard_map/all_to_all | solution.py:72
  151.4 28.8 %collective-permute-start.1 = (bf16[1,64,2560]{2,1,0:T(8,128)(2,1)S(1)}, bf16[1,64,2560]{2,1,0:T(8,128)(2,1)S(1)}, u32[]{:S(2)}, u32[]{:S(2)}) collective-permute-start(bf16[1,64,2560]{2,1,0:T(8,128)(2,1)S(1)} %fusion.51), channel_id=1, source_target_pairs={{4,0},{8,4},{12,8},{16,12},{20,16},{24,20},{28,24},{0,28},{5,1},{9... | collective-permute-start | bytes 983048 | tf_op jit(solution)/shard_map/ppermute | solution.py:12
  173.2 4.5 %copy-start.5 = (bf16[1,64,2560]{2,1,0:T(8,128)(2,1)S(1)}, bf16[1,64,2560]{2,1,0:T(8,128)(2,1)}, u32[]{:S(2)}) copy-start(bf16[1,64,2560]{2,1,0:T(8,128)(2,1)} %param.14) | copy-start | bytes 983044
  173.2 19.0 %copy-start.1 = (bf16[1,2560,16]{1,2,0:T(8,128)(2,1)S(1)}, bf16[1,2560,16]{1,2,0:T(8,128)(2,1)}, u32[]{:S(2)}) copy-start(bf16[1,2560,16]{1,2,0:T(8,128)(2,1)} %param.19) | copy-start | bytes 245764
  177.8 13.0 %collective-permute-start = (bf16[1,64,2560]{2,1,0:T(8,128)(2,1)S(1)}, bf16[1,64,2560]{2,1,0:T(8,128)(2,1)S(1)}, u32[]{:S(2)}, u32[]{:S(2)}) collective-permute-start(bf16[1,64,2560]{2,1,0:T(8,128)(2,1)S(1)} %fusion.48), channel_id=1, source_target_pairs={{28,0},{0,4},{4,8},{8,12},{12,16},{16,20},{20,24},{24,28},{29,1},{... | collective-permute-start | bytes 983048 | tf_op jit(solution)/shard_map/ppermute | solution.py:12
where the time goes:
time: 193 us; the launch traced here: 192 us
  local copies, waits for them, and re-layouts  49.8 us (26%)
  matrix products  48.2 us (25%)
  waiting for transfers between devices  40.6 us (21%)
  other arithmetic  28.3 us (15%)
  starting transfers between devices  24.1 us (12%)
    dot_general x2, matrix products, apply_experts(): jnp.einsum('slcd,ldf->slcf', rows, up_w, preferred_element_type=jnp.float32)  24.7 us
    dot_general x2, matrix products, apply_experts(): jnp.einsum('slcf,lfd->slcd', hidden, down_w, preferred_element_type=jnp.f...  23 us
    all_to_all x2, waiting for transfers between devices, dispatch_single(): lax.all_to_all(send, 'expert', split_axis=0, concat_axis=0, tiled=True)  20.3 us
    gather x2, local copies, waits for them, and re-layouts, finish(): picked = jnp.take(returned.reshape(-1, width), target, axis=0)  11.2 us
    ppermute x2, waiting for transfers between devices, shifted(): return lax.ppermute(block, axis, route)  10.6 us
    convert_element_type x2, local copies, waits for them, and re-layouts, finish(): picked = picked.reshape(tokens_here, choose, width).astype(jnp.float32)  10.1 us
    all_to_all x2, waiting for transfers between devices, run_single(): lax.all_to_all(apply_experts(rows, up_w, down_w), 'expert', split_axis=0,...  9.74 us
    reduce_sum x2, other arithmetic, finish(): combined = jnp.sum(gates[:, :, None] * picked, axis=1)  8.94 us
  transfers between devices with their start and end apart: 6, of which 5 were waited for; matrix products, arithmetic and copies ran while one was open for 55% of the time, Pallas kernels for 0%

commit v1 on v0

v1 whole, which is shorter than its diff:
```python
import jax
import jax.numpy as jnp
from jax import lax
from jax.sharding import PartitionSpec as P

CAP = 32


def shifted(block, axis, distance):
    devices = range(lax.axis_size(axis))
    route = [((i - distance) % len(devices), i) for i in devices]
    return lax.ppermute(block, axis, route)


def layer(x, ids, gain, table, up_w, down_w):
    here, width = x.shape
    experts = table.shape[1]
    local = up_w.shape[0]
    owners = experts // local
    xf = x.astype(jnp.float32)
    normed = (xf * lax.rsqrt(jnp.mean(xf * xf, axis=-1, keepdims=True) + 1e-06) * gain).astype(
        jnp.bfloat16
    )
    logits = jnp.dot(normed, table, preferred_element_type=jnp.float32)
    onehot = ids[:, :, None] == jnp.arange(experts, dtype=jnp.int32)[None, None, :]
    chosen = jnp.any(onehot, axis=1)
    score = jnp.where(chosen, jax.nn.sigmoid(logits), 0.0)
    gates = score / jnp.sum(score, axis=-1, keepdims=True)
    everyone = lax.all_gather(normed, "expert", axis=0, tiled=True)
    weights = lax.all_to_all(
        gates.reshape(here, owners, local).transpose(1, 0, 2), "expert", 0, 0, tiled=False
    ).reshape(owners, here, local)
    taken = (weights > 0).astype(jnp.float32)
    lower = (jnp.arange(here)[:, None] > jnp.arange(here)[None, :]).astype(jnp.float32)
    slot = jnp.einsum("tu,oul->otl", lower, taken)
    place = (
        (slot[:, :, :, None] == jnp.arange(CAP, dtype=jnp.float32)) & (weights > 0)[..., None]
    )
    hot = place.astype(jnp.bfloat16)
    rows = jnp.einsum(
        "otlc,otd->locd",
        hot,
        everyone.reshape(owners, here, width),
        preferred_element_type=jnp.float32,
    ).astype(jnp.bfloat16)
    rows = rows.reshape(local, owners * CAP, width)
    up_h = jnp.einsum("lcd,ldf->lcf", rows, up_w, preferred_element_type=jnp.float32)
    hidden = jax.nn.silu(up_h).astype(jnp.bfloat16)
    out = jnp.einsum("lcf,lfd->lcd", hidden, down_w, preferred_element_type=jnp.float32)
    row_gate = jnp.einsum("otlc,otl->loc", place.astype(jnp.float32), weights)
    scaled = (out * (2.5 * row_gate).reshape(local, owners * CAP, 1)).astype(jnp.bfloat16)
    part = jnp.einsum(
        "otlc,locd->otd",
        hot,
        scaled.reshape(local, owners, CAP, width),
        preferred_element_type=jnp.float32,
    ).astype(jnp.bfloat16)
    mine = lax.psum_scatter(part, "expert", scatter_dimension=0, tiled=True)[0]
    return (xf + mine.astype(jnp.float32)).astype(jnp.bfloat16)


def per_device(up_in, down_in, up_ids, down_ids, norm_gain, router, w_up, w_down):
    args = (norm_gain[0], router[0], w_up[0], w_down[0])
    up = layer(up_in[0], up_ids[0], *args)
    down = layer(down_in[0], down_ids[0], *args)
    return (shifted(up[None], "pipe", 1), shifted(down[None], "pipe", -1))


def solution(mesh):
    token = P("pipe", "expert", None)
    placed = (
        token,
        token,
        token,
        token,
        P("pipe", None),
        P("pipe", None, None),
        P("pipe", "expert", None, None),
        P("pipe", "expert", None, None),
    )
    return jax.shard_map(
        per_device, mesh=mesh, in_specs=placed, out_specs=(token, token), check_vma=False
    )
```

time: 193 us -> 140 us (0.73)
  local copies, waits for them, and re-layouts: 49.8 us -> 4.92 us
  other arithmetic: 28.3 us -> 9.52 us
  between operations: 1.05 us -> 14 us
  starting transfers between devices: 24.1 us -> 13.6 us
  matrix products: 48.2 us -> 58.1 us
    all_to_all x4 -> x2, waiting for transfers between devices: 30 us -> 4.38 us  [layer(): lax.all_to_all(gates.reshape(here, owners, local).transpose(1, 0, 2), 'ex...]
    gather x14 -> x0, local copies, waits for them, and re-layouts: 23.3 us -> none  [the longest x2 11.2 us: finish(): picked = jnp.take(returned.reshape(-1, width), target, axis=0)]
    reduce_scatter x0 -> x2, waiting for transfers between devices: none -> 21.4 us  [layer(): mine = lax.psum_scatter(part, 'expert', scatter_dimension=0, tiled=True)[0]]
    convert_element_type x4 -> x2, local copies, waits for them, and re-layouts: 13.5 us -> 0.45 us  [layer(): rows = jnp.einsum('otlc,otd->locd', hot, everyone.reshape(owners, here, w...]
    reduce_sum x8 -> x2, other arithmetic: 11.5 us -> 2.35 us  [layer(): jnp.mean(xf * xf, axis=-1, keepdims=True) + 1e-06]
    all_to_all x4 -> x2, starting transfers between devices: 16.3 us -> 7.44 us  [layer(): lax.all_to_all(gates.reshape(here, owners, local).transpose(1, 0, 2), 'ex...]
    scatter x2 -> x0, local copies, waits for them, and re-layouts: 5.82 us -> none  [layer_route(): source_row = jnp.zeros((experts * CAP,), jnp.int32).at[target].set(token_of)]
    dot_general x6 -> x12, matrix products: 48.2 us -> 53.8 us  [the longest x2 24.8 us: layer(): jnp.einsum('lcd,ldf->lcf', rows, up_w, preferred_element_type=jnp.float32)]
  transfers between devices with their start and end apart: 6 -> 8, of which waited for: 5 -> 5; matrix products, arithmetic and copies ran while one was open for 55% -> 47% of each run, Pallas kernels for 0% -> 0%
where the time goes in v1:
time: 140 us; the launch traced here: 139 us
  matrix products  58.1 us (42%)
  waiting for transfers between devices  38.9 us (28%)
  between operations  14 us (10%)
  starting transfers between devices  13.6 us (10%)
  other arithmetic  9.52 us (7%)
  local copies, waits for them, and re-layouts  4.92 us (4%)
    dot_general x2, matrix products, layer(): jnp.einsum('lcd,ldf->lcf', rows, up_w, preferred_element_type=jnp.float32)  24.8 us
    dot_general x2, matrix products, layer(): jnp.einsum('lcf,lfd->lcd', hidden, down_w, preferred_element_type=jnp.flo...  23.5 us
    reduce_scatter x2, waiting for transfers between devices, layer(): mine = lax.psum_scatter(part, 'expert', scatter_dimension=0, tiled=True)[0]  21.4 us
    ppermute x2, waiting for transfers between devices, shifted(): return lax.ppermute(block, axis, route)  10.7 us
    all_to_all x2, starting transfers between devices, layer(): lax.all_to_all(gates.reshape(here, owners, local).transpose(1, 0, 2), 'ex...  7.44 us
    ppermute x2, starting transfers between devices, shifted(): return lax.ppermute(block, axis, route)  5.81 us
    all_to_all x2, waiting for transfers between devices, layer(): lax.all_to_all(gates.reshape(here, owners, local).transpose(1, 0, 2), 'ex...  4.38 us
    unnamed x2, matrix products  4.27 us
  transfers between devices with their start and end apart: 8, of which 5 were waited for; matrix products, arithmetic and copies ran while one was open for 47% of the time, Pallas kernels for 0%

profile of v1, /device:TPU:0, one launch (start us, length us, event | category | flops | bytes accessed | tf_op | source)
XLA Modules:
  0.0 139.0 jit_solution(7580024494856796830)
XLA Ops:
  7.2 1.2 fusion.32
  8.5 1.1 fusion.35
  9.6 0.7 reduce
  10.4 2.1 %fusion.34 = (bf16[64,2560]{1,0:T(8,128)(2,1)}, bf16[64,2560]{1,0:T(8,128)(2,1)}) fusion(bf16[1,64,2560]{2,1,0:T(8,128)(2,1)} %param.9, f32[64]{0:T(128)S(1)} %get-tuple-element.8, f32[2560]{0:T(1024)S(1)} %reduce, f32[64]{0:T(128)S(1)} %get-tuple-element.9, bf16[1,64,2560]{2,1,0:T(8,128)(2,1)} %param.8), kind=kLoop, calls=%fused_computation.44 | loop fusion | flops 1310720 | bytes 1321472 | tf_op jit(solution)/shard_map/convert_element_type | solution.py:21
  12.5 0.7 copy.48
  13.2 1.3 fusion.70
  14.5 0.7 reshape.112
  15.2 4.2 %all-to-all-start.1 = ((f32[4,1,256]{2,1,0:T(1,128)}), f32[4,1,256]{2,1,0:T(1,128)S(1)}, u32[]{:S(2)}, u32[]{:S(2)}) async-start(f32[4,1,256]{2,1,0:T(1,128)} %reshape.112), calls=%async_computation.2 | async-start | bytes 8192 | tf_op jit(solution)/shard_map/all_to_all | solution.py:30
  19.4 0.7 all-gather.3.cloned.1.call-update
  20.2 0.3 fusion.69
  20.5 0.7 reshape.110
  21.2 2.0 %all-to-all-done.1 = f32[4,1,256]{2,1,0:T(1,128)S(1)} async-done(((f32[4,1,256]{2,1,0:T(1,128)}), f32[4,1,256]{2,1,0:T(1,128)S(1)}, u32[]{:S(2)}, u32[]{:S(2)}) %all-to-all-start.1) | async-done | bytes 4128 | tf_op jit(solution)/shard_map/all_to_all | solution.py:30
  23.2 3.2 %all-to-all-start = ((f32[4,1,256]{2,1,0:T(1,128)}), f32[4,1,256]{2,1,0:T(1,128)S(1)}, u32[]{:S(2)}, u32[]{:S(2)}) async-start(f32[4,1,256]{2,1,0:T(1,128)} %reshape.110), calls=%async_computation | async-start | bytes 8192 | tf_op jit(solution)/shard_map/all_to_all | solution.py:30
  26.5 0.6 broadcast.76
  27.1 0.7 reduce.2
  27.7 0.1 reshape.113
  27.8 2.4 %all-to-all-done = f32[4,1,256]{2,1,0:T(1,128)S(1)} async-done(((f32[4,1,256]{2,1,0:T(1,128)}), f32[4,1,256]{2,1,0:T(1,128)S(1)}, u32[]{:S(2)}, u32[]{:S(2)}) %all-to-all-start) | async-done | bytes 4128 | tf_op jit(solution)/shard_map/all_to_all | solution.py:30
  30.2 0.7 reduce.1
  30.8 0.1 reshape.111
  31.0 0.1 convolution_bitcast_fusion.2
  31.2 0.2 fusion.54
  31.3 0.1 mul.113
  31.4 0.1 convolution_bitcast_fusion.3
  31.6 0.1 fusion.52
  31.6 0.2 fusion.56
  31.8 0.1 mul.101
  31.9 1.7 %all-gather.5.cloned.1.call-done = bf16[256,2560]{1,0:T(8,128)(2,1)} async-done(((bf16[64,2560]{1,0:T(8,128)(2,1)}), bf16[256,2560]{1,0:T(8,128)(2,1)}) %all-gather.5.cloned.1.call-update) | async-done | bytes 1310736 | tf_op jit(solution)/shard_map/all_gather | solution.py:29
  33.6 2.1 %fusion.72 = f32[4,2560,128]{1,2,0:S(1)} fusion(bf16[4,64,2560]{2,1,0:T(8,128)(2,1)} %bitcast.137, pred[4,64,128]{1,2,0:T(32,128)(4,1)S(1)} %bitcast.140), kind=kOutput, calls=%fused_computation.93 | convolution fusion | flops 167772160 | bytes 6586368
  35.7 0.3 convert_bitcast_fusion
  36.1 0.2 copy.22
  36.3 12.3 %multiply_convert_fusion.2 = bf16[4,128,1152]{2,1,0:T(8,128)(2,1)S(1)} fusion(bf16[4,128,2560]{2,1,0:T(8,128)(2,1)S(1)} %bitcast.135, bf16[1,4,2560,1152]{3,2,1,0:T(8,128)(2,1)} %param.14), kind=kOutput, calls=%fused_computation.18 | convolution fusion | flops 3022848000 | bytes 27394048 | tf_op jit(solution)/shard_map/lcd,ldf->lcf/dot_general | solution.py:47
  48.6 11.7 %multiply_convert_fusion = bf16[4,128,2560]{2,1,0:T(8,128)(2,1)S(1)} fusion(bf16[4,128,1152]{2,1,0:T(8,128)(2,1)S(1)} %multiply_convert_fusion.2, bf16[1,4,1152,2560]{3,2,1,0:T(8,128)(2,1)} %param.15, f32[4,128]{1,0:T(4,128)S(1)} %mul.113), kind=kOutput, calls=%fused_computation.8 | convolution fusion | flops 3022520320 | bytes 27396096 | tf_op jit(solution)/shard_map/lcf,lfd->lcd/dot_general | solution.py:49
  60.3 1.7 %fusion.13 = bf16[4,64,2560]{2,1,0:T(8,128)(2,1)} fusion(bf16[4,4,32,2560]{3,2,1,0:T(8,128)(2,1)S(1)} %bitcast.133, f32[4,64,4]{1,2,0:T(4,128)S(1)} %convolution_bitcast_fusion.2, pred[4,64,4]{1,2,0:T(4,128)(4,1)S(1)} %broadcast_compare_fusion), kind=kOutput, calls=%fused_computation.13 | convolution fusion | flops 168493056 | bytes 3937280 | tf_op jit(solution)/shard_map/otlc,locd->otd/dot_general | solution.py:52
  62.0 0.2 reduce-scatter.3.cloned.1.call-start
  62.2 2.1 %fusion.71 = f32[4,2560,128]{1,2,0:S(1)} fusion(bf16[4,64,2560]{2,1,0:T(8,128)(2,1)} %bitcast.138, pred[4,64,128]{1,2,0:T(32,128)(4,1)S(1)} %bitcast.139), kind=kOutput, calls=%fused_computation.92 | convolution fusion | flops 167772160 | bytes 6586368
  64.4 0.3 convert_bitcast_fusion.1
  64.7 0.2 copy.20
  64.9 12.5 %multiply_convert_fusion.3 = bf16[4,128,1152]{2,1,0:T(8,128)(2,1)S(1)} fusion(bf16[4,128,2560]{2,1,0:T(8,128)(2,1)S(1)} %bitcast.136, bf16[1,4,2560,1152]{3,2,1,0:T(8,128)(2,1)} %param.14), kind=kOutput, calls=%fused_computation.19 | convolution fusion | flops 3022848000 | bytes 27394048 | tf_op jit(solution)/shard_map/lcd,ldf->lcf/dot_general | solution.py:47
  77.5 11.8 %multiply_convert_fusion.1 = bf16[4,128,2560]{2,1,0:T(8,128)(2,1)S(1)} fusion(bf16[4,128,1152]{2,1,0:T(8,128)(2,1)S(1)} %multiply_convert_fusion.3, bf16[1,4,1152,2560]{3,2,1,0:T(8,128)(2,1)} %param.15, f32[4,128]{1,0:T(4,128)S(1)} %mul.101), kind=kOutput, calls=%fused_computation.9 | convolution fusion | flops 3022520320 | bytes 27396096 | tf_op jit(solution)/shard_map/lcf,lfd->lcd/dot_general | solution.py:49
  89.3 1.6 %fusion.12 = bf16[4,64,2560]{2,1,0:T(8,128)(2,1)} fusion(bf16[4,4,32,2560]{3,2,1,0:T(8,128)(2,1)S(1)} %bitcast.134, f32[4,64,4]{1,2,0:T(4,128)S(1)} %convolution_bitcast_fusion.3, pred[4,64,4]{1,2,0:T(4,128)(4,1)S(1)} %broadcast_compare_fusion.1), kind=kOutput, calls=%fused_computation.12 | convolution fusion | flops 168493056 | bytes 3937280 | tf_op jit(solution)/shard_map/otlc,locd->otd/dot_general | solution.py:52
  91.0 1.1 fusion.43
  92.1 4.3 %collective-permute-start.1 = (bf16[1,64,2560]{2,1,0:T(8,128)(2,1)S(1)}, bf16[1,64,2560]{2,1,0:T(8,128)(2,1)S(1)}, u32[]{:S(2)}, u32[]{:S(2)}) collective-permute-start(bf16[1,64,2560]{2,1,0:T(8,128)(2,1)S(1)} %fusion.43), channel_id=1, source_target_pairs={{4,0},{8,4},{12,8},{16,12},{20,16},{24,20},{28,24},{0,28},{5,1},{9... | collective-permute-start | bytes 983048 | tf_op jit(solution)/shard_map/ppermute | solution.py:12
  96.4 21.4 %reduce-scatter.3.cloned.1.call-done = bf16[1,64,2560]{2,1,0:T(8,128)(2,1)} async-done(((bf16[4,64,2560]{2,1,0:T(8,128)(2,1)}), bf16[1,64,2560]{2,1,0:T(8,128)(2,1)}) %reduce-scatter.3.cloned.1.call-update) | async-done | bytes 327696 | tf_op jit(solution)/shard_map/reduce_scatter | solution.py:58
  117.7 1.0 fusion.40
  118.8 1.5 %collective-permute-start = (bf16[1,64,2560]{2,1,0:T(8,128)(2,1)S(1)}, bf16[1,64,2560]{2,1,0:T(8,128)(2,1)S(1)}, u32[]{:S(2)}, u32[]{:S(2)}) collective-permute-start(bf16[1,64,2560]{2,1,0:T(8,128)(2,1)S(1)} %fusion.40), channel_id=1, source_target_pairs={{28,0},{0,4},{4,8},{8,12},{12,16},{16,20},{20,24},{24,28},{29,1},{... | collective-permute-start | bytes 983048 | tf_op jit(solution)/shard_map/ppermute | solution.py:12
  120.3 10.7 %collective-permute-done = bf16[1,64,2560]{2,1,0:T(8,128)(2,1)S(1)} collective-permute-done((bf16[1,64,2560]{2,1,0:T(8,128)(2,1)S(1)}, bf16[1,64,2560]{2,1,0:T(8,128)(2,1)S(1)}, u32[]{:S(2)}, u32[]{:S(2)}) %collective-permute-start) | collective-permute-done | bytes 327712 | tf_op jit(solution)/shard_map/ppermute | solution.py:12
  131.0 0.7 copy.56
  131.7 0.7 copy.57
  (32 shorter events, 0.4 us)
Async XLA Ops:
  7.2 6.1 %copy-start = (bf16[1,2560,16]{1,2,0:T(8,128)(2,1)S(1)}, bf16[1,2560,16]{1,2,0:T(8,128)(2,1)}, u32[]{:S(2)}) copy-start(bf16[1,2560,16]{1,2,0:T(8,128)(2,1)} %param.13) | copy-start | bytes 245764
  7.2 13.0 %copy-start.3 = (bf16[1,64,2560]{2,1,0:T(8,128)(2,1)S(1)}, bf16[1,64,2560]{2,1,0:T(8,128)(2,1)}, u32[]{:S(2)}) copy-start(bf16[1,64,2560]{2,1,0:T(8,128)(2,1)} %param.8) | copy-start | bytes 983044
  7.2 13.0 %copy-start.4 = (s32[1,64,6]{1,0,2:T(1,128)S(1)}, s32[1,64,6]{1,0,2:T(1,128)}, u32[]{:S(2)}) copy-start(s32[1,64,6]{1,0,2:T(1,128)} %param.10) | copy-start | bytes 4612
  7.2 26.4 %all-gather.5.cloned.1.call-start = ((), (), s32[]{:S(2)}) async-start(), calls=%async_computation.6 | async-start | bytes 1638400 | tf_op jit(solution)/shard_map/all_gather | solution.py:29
  15.2 8.0 %all-to-all-start.1 = ((f32[4,1,256]{2,1,0:T(1,128)}), f32[4,1,256]{2,1,0:T(1,128)S(1)}, u32[]{:S(2)}, u32[]{:S(2)}) async-start(f32[4,1,256]{2,1,0:T(1,128)} %reshape.112), calls=%async_computation.2 | async-start | bytes 8192 | tf_op jit(solution)/shard_map/all_to_all | solution.py:30
  19.4 42.8 %all-gather.3.cloned.1.call-start = ((), (), s32[]{:S(2)}) async-start(), calls=%async_computation.4 | async-start | bytes 1638400 | tf_op jit(solution)/shard_map/all_gather | solution.py:29
  23.2 7.0 %all-to-all-start = ((f32[4,1,256]{2,1,0:T(1,128)}), f32[4,1,256]{2,1,0:T(1,128)S(1)}, u32[]{:S(2)}, u32[]{:S(2)}) async-start(f32[4,1,256]{2,1,0:T(1,128)} %reshape.110), calls=%async_computation | async-start | bytes 8192 | tf_op jit(solution)/shard_map/all_to_all | solution.py:30
  26.4 64.6 %reduce-scatter.5.cloned.1.call-start = ((), (), s32[]{:S(2)}) async-start(), calls=%async_computation.7 | async-start | bytes 1638400 | tf_op jit(solution)/shard_map/reduce_scatter | solution.py:58
  62.0 55.8 %reduce-scatter.3.cloned.1.call-start = ((), (), s32[]{:S(2)}) async-start(), calls=%async_computation.5 | async-start | bytes 1638400 | tf_op jit(solution)/shard_map/reduce_scatter | solution.py:58
  89.3 1.7 %copy-start.2 = (bf16[1,64,2560]{2,1,0:T(8,128)(2,1)S(1)}, bf16[1,64,2560]{2,1,0:T(8,128)(2,1)}, u32[]{:S(2)}) copy-start(bf16[1,64,2560]{2,1,0:T(8,128)(2,1)} %param.9) | copy-start | bytes 983044
  89.3 43.1 %copy-start.1 = (bf16[1,2560,16]{1,2,0:T(8,128)(2,1)S(1)}, bf16[1,2560,16]{1,2,0:T(8,128)(2,1)}, u32[]{:S(2)}) copy-start(bf16[1,2560,16]{1,2,0:T(8,128)(2,1)} %param.13) | copy-start | bytes 245764
  92.1 28.2 %collective-permute-start.1 = (bf16[1,64,2560]{2,1,0:T(8,128)(2,1)S(1)}, bf16[1,64,2560]{2,1,0:T(8,128)(2,1)S(1)}, u32[]{:S(2)}, u32[]{:S(2)}) collective-permute-start(bf16[1,64,2560]{2,1,0:T(8,128)(2,1)S(1)} %fusion.43), channel_id=1, source_target_pairs={{4,0},{8,4},{12,8},{16,12},{20,16},{24,20},{28,24},{0,28},{5,1},{9... | collective-permute-start | bytes 983048 | tf_op jit(solution)/shard_map/ppermute | solution.py:12
  118.8 12.2 %collective-permute-start = (bf16[1,64,2560]{2,1,0:T(8,128)(2,1)S(1)}, bf16[1,64,2560]{2,1,0:T(8,128)(2,1)S(1)}, u32[]{:S(2)}, u32[]{:S(2)}) collective-permute-start(bf16[1,64,2560]{2,1,0:T(8,128)(2,1)S(1)} %fusion.40), channel_id=1, source_target_pairs={{28,0},{0,4},{4,8},{8,12},{12,16},{16,20},{20,24},{24,28},{29,1},{... | collective-permute-start | bytes 983048 | tf_op jit(solution)/shard_map/ppermute | solution.py:12
Sparse Core Ops, SparseCore 0:
  12.6 20.9 all-gather.4
  35.7 18.2 all-gather.2
  62.1 26.5 reduce-scatter.4
  91.2 26.5 reduce-scatter.2

commit v2 on v1

v2 whole, which is shorter than its diff:
```python
import functools

import jax
import jax.numpy as jnp
from jax import lax
from jax.experimental import pallas as pl
from jax.experimental.pallas import tpu as pltpu
from jax.sharding import PartitionSpec as P

CAP = 32
EXTRA = 128
MESH = pl.DeviceIdType.MESH
BF16, F32 = jnp.bfloat16, jnp.float32


def kernel(
    owners,
    pipes,
    columns,
    up_ref,
    down_ref,
    up_ids,
    down_ids,
    gain_ref,
    router_ref,
    w_up,
    w_down,
    up_out,
    down_out,
    tokens,
    rows,
    hidden,
    spread,
    scaled,
    part,
    paired,
    crossed,
    final,
    wu,
    wd,
    wu_sem,
    wd_sem,
    own_send,
    own_recv,
    far_send,
    far_recv,
    fwd_send,
    fwd_recv,
    pair_send,
    pair_recv,
    cross_send,
    cross_recv,
    out_send,
    out_recv,
):
    chips = owners // 2
    here, width = up_ref.shape[1:]
    experts = router_ref.shape[2]
    local = w_up.shape[1]
    slots = owners * CAP
    everyone = owners * here
    chunks = width // columns
    pipe, me = lax.axis_index("pipe"), lax.axis_index("expert")
    chip, core = me // 2, lax.rem(me, 2)
    other = 1 - core
    sibling = {"expert": chip * 2 + other}
    above = {"pipe": lax.rem(pipe + 1, pipes)}
    below = {"pipe": lax.rem(pipe + pipes - 1, pipes)}

    def across(k):
        return lax.rem(chip + k, chips)

    def facing(k):
        return {"expert": across(k) * 2 + core}

    def cols(c):
        return pl.ds(pl.multiple_of(c * columns, columns), columns)

    def load_up(l):
        return pltpu.make_async_copy(w_up.at[0, l], wu.at[l], wu_sem.at[l])

    def load_down(c):
        return pltpu.make_async_copy(
            w_down.at[0, :, :, cols(c)], wd.at[:, :, cols(c)], wd_sem.at[c]
        )

    def remote(src, dst, send, recv, to):
        return pltpu.make_async_remote_copy(
            src_ref=src,
            dst_ref=dst,
            send_sem=send,
            recv_sem=recv,
            device_id=to,
            device_id_type=MESH,
        )

    def own_copy(d):
        block = tokens.at[d, core, chip]
        return remote(block, block, own_send.at[d], own_recv.at[d], sibling)

    def far_copy(d, k):
        block = tokens.at[d, core, chip]
        return remote(block, block, far_send.at[d, k - 1], far_recv.at[d, k - 1], facing(k))

    def fwd_copy(d, k):
        block = tokens.at[d, core, across(chips - k)]
        return remote(block, block, fwd_send.at[d, k - 1], fwd_recv.at[d, k - 1], sibling)

    def pair_copy(d, c):
        return remote(
            part.at[d, other, :, :, cols(c)],
            paired.at[d, :, :, cols(c)],
            pair_send.at[d, c],
            pair_recv.at[d, c],
            sibling,
        )

    def cross_copy(d, c, k):
        return remote(
            part.at[d, core, across(k), :, cols(c)],
            crossed.at[d, k - 1, :, cols(c)],
            cross_send.at[d, c, k - 1],
            cross_recv.at[d, c, k - 1],
            facing(k),
        )

    def out_copy(d, c):
        target, to = ((up_out, above), (down_out, below))[d]
        return remote(
            final.at[d, :, cols(c)],
            target.at[0, :, cols(c)],
            out_send.at[d, c],
            out_recv.at[d, c],
            to,
        )

    for l in range(local):
        load_up(l).start()

    barrier = pltpu.get_barrier_semaphore()
    partners = [sibling, above, below] + [facing(k) for k in range(1, chips)]
    for partner in partners:
        pl.semaphore_signal(barrier, inc=1, device_id=partner, device_id_type=MESH)

    def route(d):
        x_ref, ids_ref = ((up_ref, up_ids), (down_ref, down_ids))[d]
        xf = x_ref[0].astype(F32)
        mean = jnp.mean(xf * xf, axis=-1, keepdims=True)
        normed = (xf * lax.rsqrt(mean + 1e-06) * gain_ref[...]).astype(BF16)
        logits = jnp.dot(normed, router_ref[0], preferred_element_type=F32)
        ids = ids_ref[0]
        lane = lax.broadcasted_iota(jnp.int32, (here, experts), 1)
        taken = jnp.zeros((here, experts), F32)
        for k in range(ids.shape[1]):
            taken = taken + jnp.where(ids[:, k : k + 1] == lane, 1.0, 0.0)
        score = taken / (1.0 + jnp.exp(-logits))
        gates = 2.5 * (score / jnp.sum(score, axis=-1, keepdims=True))
        high = gates.astype(BF16)
        low = (gates - high.astype(F32)).astype(BF16)
        earlier = lax.broadcasted_iota(jnp.int32, (here, here), 0) > lax.broadcasted_iota(
            jnp.int32, (here, here), 1
        )
        slot = jnp.dot(
            jnp.where(earlier, 1.0, 0.0).astype(BF16),
            taken.astype(BF16),
            preferred_element_type=F32,
        )
        slot = jnp.where(taken > 0.0, slot, -1024.0).astype(BF16)
        from_lane = lax.broadcasted_iota(jnp.int32, (experts, EXTRA), 0)
        to_lane = lax.broadcasted_iota(jnp.int32, (experts, EXTRA), 1)
        extra = jnp.zeros((here, EXTRA), F32)
        for place, value in enumerate((high, low, slot)):
            move = jnp.where(from_lane + place * experts == to_lane, 1.0, 0.0).astype(BF16)
            extra = extra + jnp.dot(value, move, preferred_element_type=F32)
        tokens[d, core, chip, :, :width] = normed
        tokens[d, core, chip, :, width:] = extra.astype(BF16)

    def find_rows(d):
        everything = tokens[d].reshape(everyone, width + EXTRA)
        extra = tokens[d, :, :, :, width:].reshape(everyone, EXTRA).astype(F32)
        lane = lax.broadcasted_iota(jnp.int32, (everyone, EXTRA), 1)
        block = lax.broadcasted_iota(jnp.int32, (everyone, slots), 0) // here
        place = lax.broadcasted_iota(jnp.int32, (everyone, slots), 1) - block * CAP

        @pl.loop(0, local)
        def _(l):
            column = 2 * experts + me * local + l
            slot = jnp.sum(jnp.where(lane == column, extra, 0.0), axis=1, keepdims=True)
            hot = jnp.where(place.astype(F32) == slot, 1.0, 0.0)
            spread[:, pl.ds(pl.multiple_of(l * slots, slots), slots)] = hot.astype(BF16)
            rows[l] = jnp.dot(
                hot.T.astype(BF16), everything, preferred_element_type=F32
            ).astype(BF16)

    def find_hidden(d):
        @pl.loop(0, local)
        def _(l):
            if d == 0:
                load_up(l).wait()
            up_h = jnp.dot(rows[l, :, :width], wu[l], preferred_element_type=F32)
            hidden[l] = (up_h / (1.0 + jnp.exp(-up_h))).astype(BF16)

    def find_part(d, c):
        if d == 0:
            load_down(c).wait()
        lane = lax.broadcasted_iota(jnp.int32, (slots, EXTRA), 1)
        for l in range(local):
            expert = me * local + l
            gate = jnp.sum(
                jnp.where(
                    (lane == expert) | (lane == expert + experts),
                    rows[l, :, width:].astype(F32),
                    0.0,
                ),
                axis=1,
                keepdims=True,
            )
            value = jnp.dot(hidden[l], wd[l, :, cols(c)], preferred_element_type=F32)
            scaled[l * slots : (l + 1) * slots, :] = (value * gate).astype(BF16)
        total = jnp.dot(spread[...], scaled[...], preferred_element_type=F32).astype(BF16)
        part[d, :, :, :, cols(c)] = total.reshape(2, chips, here, columns)
        pair_copy(d, c).start()

    def cross(d, c):
        pair_copy(d, c).wait_recv()
        for k in range(1, chips):
            q = across(k)
            both = part[d, core, q, :, cols(c)].astype(F32) + paired[d, q, :, cols(c)].astype(F32)
            part[d, core, q, :, cols(c)] = both.astype(BF16)
            cross_copy(d, c, k).start()

    def finish(d, c):
        x_ref = (up_ref, down_ref)[d]
        total = x_ref[0, :, cols(c)].astype(F32)
        total = total + part[d, core, chip, :, cols(c)].astype(F32)
        total = total + paired[d, chip, :, cols(c)].astype(F32)
        for k in range(1, chips):
            cross_copy(d, c, k).wait_recv()
            total = total + crossed[d, k - 1, :, cols(c)].astype(F32)
        final[d, :, cols(c)] = total.astype(BF16)
        out_copy(d, c).start()

    def forward(d):
        for k in range(1, chips):
            far_copy(d, k).wait_recv()
            fwd_copy(d, k).start()

    route(0)
    pl.semaphore_wait(barrier, len(partners))
    for k in range(1, chips):
        far_copy(0, k).start()
    own_copy(0).start()
    for c in range(chunks):
        load_down(c).start()
    route(1)
    own_copy(1).start()
    forward(0)
    for k in range(1, chips):
        far_copy(1, k).start()

    own_copy(0).wait_recv()
    for k in range(1, chips):
        fwd_copy(0, k).wait_recv()
    find_rows(0)
    find_hidden(0)

    @pl.loop(0, chunks)
    def _(c):
        find_part(0, c)

        @pl.when(c >= 1)
        def _():
            cross(0, c - 1)

        @pl.when(c == chunks - 2)
        def _():
            forward(1)

    cross(0, chunks - 1)
    own_copy(1).wait_recv()
    for k in range(1, chips):
        fwd_copy(1, k).wait_recv()
    find_rows(1)
    find_hidden(1)

    @pl.loop(0, chunks)
    def _(c):
        find_part(1, c)

        @pl.when(c >= 1)
        def _():
            cross(1, c - 1)

        finish(0, c)

    cross(1, chunks - 1)

    @pl.loop(0, chunks)
    def _(c):
        finish(1, c)

    for d in range(2):
        own_copy(d).wait_send()
        for k in range(1, chips):
            far_copy(d, k).wait_send()
            fwd_copy(d, k).wait_send()

        @pl.loop(0, chunks)
        def _(c):
            pair_copy(d, c).wait_send()
            for k in range(1, chips):
                cross_copy(d, c, k).wait_send()
            out_copy(d, c).wait_send()
            out_copy(d, c).wait_recv()


def solution(mesh):
    owners, pipes = mesh.shape["expert"], mesh.shape["pipe"]
    chips = owners // 2
    token = P("pipe", "expert", None)

    def per_device(up_in, down_in, up_ids, down_ids, norm_gain, router, w_up, w_down):
        here, width = up_in.shape[1:]
        local, _, inner = w_up.shape[1:]
        slots = owners * CAP
        columns = 512
        chunks = width // columns
        dma = pltpu.SemaphoreType.DMA
        shape = jax.ShapeDtypeStruct(up_in.shape, BF16)
        vmem = pl.BlockSpec(memory_space=pltpu.VMEM)
        hbm = pl.BlockSpec(memory_space=pl.ANY)
        return pl.pallas_call(
            functools.partial(kernel, owners, pipes, columns),
            out_shape=(shape, shape),
            in_specs=[vmem] * 6 + [hbm] * 2,
            out_specs=(hbm, hbm),
            scratch_shapes=[
                pltpu.VMEM((2, 2, chips, here, width + EXTRA), BF16),
                pltpu.VMEM((local, slots, width + EXTRA), BF16),
                pltpu.VMEM((local, slots, inner), BF16),
                pltpu.VMEM((owners * here, local * slots), BF16),
                pltpu.VMEM((local * slots, columns), BF16),
                pltpu.VMEM((2, 2, chips, here, width), BF16),
                pltpu.VMEM((2, chips, here, width), BF16),
                pltpu.VMEM((2, chips - 1, here, width), BF16),
                pltpu.VMEM((2, here, width), BF16),
                pltpu.VMEM((local, width, inner), BF16),
                pltpu.VMEM((local, inner, width), BF16),
                dma((local,)),
                dma((chunks,)),
                dma((2,)),
                dma((2,)),
                dma((2, chips - 1)),
                dma((2, chips - 1)),
                dma((2, chips - 1)),
                dma((2, chips - 1)),
                dma((2, chunks)),
                dma((2, chunks)),
                dma((2, chunks, chips - 1)),
                dma((2, chunks, chips - 1)),
                dma((2, chunks)),
                dma((2, chunks)),
            ],
            compiler_params=pltpu.CompilerParams(
                collective_id=0, has_side_effects=True, vmem_limit_bytes=63 * 1024 * 1024
            ),
        )(up_in, down_in, up_ids, down_ids, norm_gain, router, w_up, w_down)

    return jax.shard_map(
        per_device,
        mesh=mesh,
        in_specs=(
            token,
            token,
            token,
            token,
            P("pipe", None),
            P("pipe", None, None),
            P("pipe", "expert", None, None),
            P("pipe", "expert", None, None),
        ),
        out_specs=(token, token),
        check_vma=False,
    )
```

time: 140 us -> 64 us (0.46)
  matrix products: 58.1 us -> 0 us
  Pallas kernels: 0 us -> 54.9 us
  waiting for transfers between devices: 38.9 us -> 0 us
  starting transfers between devices: 13.6 us -> 0 us
  between operations: 14 us -> 0.64 us
  other arithmetic: 9.52 us -> 0 us
  local copies, waits for them, and re-layouts: 4.92 us -> 8.19 us
    pallas_call x0 -> x1, Pallas kernels: none -> 54.9 us  [per_device(): pl.pallas_call(functools.partial(kernel, owners, pipes, columns), out_sha...]
    dot_general x12 -> x0, matrix products: 53.8 us -> none  [the longest x2 24.8 us: layer(): jnp.einsum('lcd,ldf->lcf', rows, up_w, preferred_element_type=jnp.float32)]
    reduce_scatter x2 -> x0, waiting for transfers between devices: 21.4 us -> none  [layer(): mine = lax.psum_scatter(part, 'expert', scatter_dimension=0, tiled=True)[0]]
    ppermute x2 -> x0, waiting for transfers between devices: 10.7 us -> none  [shifted(): return lax.ppermute(block, axis, route)]
    all_to_all x2 -> x0, starting transfers between devices: 7.44 us -> none  [layer(): lax.all_to_all(gates.reshape(here, owners, local).transpose(1, 0, 2), 'ex...]
    ppermute x2 -> x0, starting transfers between devices: 5.81 us -> none  [shifted(): return lax.ppermute(block, axis, route)]
    convert_element_type x5 -> x0, other arithmetic: 4.9 us -> none  [the longest x1 2.12 us: layer(): (xf * lax.rsqrt(jnp.mean(xf * xf, axis=-1, keepdims=True) + 1e-06) * gain...]
    unnamed x18 -> x5, local copies, waits for them, and re-layouts: 3.71 us -> 8.19 us
  transfers between devices with their start and end apart: 8 -> 0, of which waited for: 5 -> 0; matrix products, arithmetic and copies ran while one was open for 47% -> 0% of each run, Pallas kernels for 0% -> 0%
where the time goes in v2:
time: 64 us; the launch traced here: 63.7 us
  Pallas kernels  54.9 us (86%)
  local copies, waits for them, and re-layouts  8.19 us (13%)
  between operations  0.64 us (1%)
    pallas_call x1, Pallas kernels, per_device(): pl.pallas_call(functools.partial(kernel, owners, pipes, columns), out_sha...  54.9 us
    unnamed x5, local copies, waits for them, and re-layouts  8.19 us

profile of v2, /device:TPU:0, one launch (start us, length us, event | category | flops | bytes accessed | tf_op | source)
XLA Modules:
  0.0 63.7 jit_solution(14413281684825095095)
XLA Ops:
  0.6 1.4 %copy.10.up_ids = s32[1,64,6]{2,1,0:T(8,128)} copy(s32[1,64,6]{1,0,2:T(1,128)} %param.10) | data formatting | bytes 3072 | tf_op args[2]
  2.0 1.4 %copy.11.down_ids = s32[1,64,6]{2,1,0:T(8,128)} copy(s32[1,64,6]{1,0,2:T(1,128)} %param.11) | data formatting | bytes 3072 | tf_op args[3]
  3.4 2.0 %copy.12.router_ref = bf16[1,2560,16]{2,1,0:T(8,128)(2,1)} copy(bf16[1,2560,16]{1,2,0:T(8,128)(2,1)} %param.13) | data formatting | bytes 163840 | tf_op args[5]
  5.4 54.9 %shard_map.95 = (bf16[1,64,2560]{2,1,0:T(8,128)(2,1)}, bf16[1,64,2560]{2,1,0:T(8,128)(2,1)}) custom-call(bf16[1,64,2560]{2,1,0:T(8,128)(2,1)} %up_ref.1, bf16[1,64,2560]{2,1,0:T(8,128)(2,1)} %down_ref.1, s32[1,64,6]{2,1,0:T(8,128)} %copy.10.up_ids, s32[1,64,6]{2,1,0:T(8,128)} %copy.11.down_ids, f32[1,2560]{1,0:T(1,128)} %gain_ref.1, ...), custom_call_target="tpu_custom_call" | custom-call | tf_op jit(solution)/shard_map/pallas_call | solution.py:332
  60.3 1.7 %copy.15 = bf16[1,64,2560]{2,1,0:T(8,128)(2,1)} copy(bf16[1,64,2560]{2,1,0:T(8,128)(2,1)} %get-tuple-element.4) | data formatting | bytes 655360
  62.0 1.7 %copy.16 = bf16[1,64,2560]{2,1,0:T(8,128)(2,1)} copy(bf16[1,64,2560]{2,1,0:T(8,128)(2,1)} %get-tuple-element.5) | data formatting | bytes 655360
